TPU v7x, 32 devices: a whole 2x2x4 slice. The times are simulated.
32 devices in a mesh: grp: 2 (over x), seq: 16 (over z, y, core).
Axes of the slice: x: 2, y: 2, z: 4, core: 2. Of those that a mesh axis runs over, the one named last changes fastest.
Arguments:
- tokens: bfloat16 [2, 131072, 768], P('grp', 'seq'), parts along dimension 0, may hold values from -36 to 36
- right_factor: bfloat16 [256, 512, 512], P('seq'), may hold values from -0.25 to 0.25
- left_factor: bfloat16 [512, 256, 256], P('seq'), may hold values from -0.375 to 0.375
- twiddle: float32 [256, 512], P('seq'), may hold values from 0.5 to 2
- norm_gain: float32 [768], replicated, may hold values from 0.1 to 1.9
- mix_gain: float32 [768], replicated, may hold values from 0.1 to 1.9
- value_weight: bfloat16 [768, 768], replicated, may hold values from -0.21875 to 0.21875
- gate_weight: bfloat16 [768, 768], replicated, may hold values from -0.21875 to 0.21875
Outputs:
- layer_out: bfloat16 [2, 131072, 768], P('grp', 'seq'), parts along dimension 0
There are 2 independent parts, one for each index of `grp`. A program takes and returns all parts, laid end to end along the dimension named above; an argument that names none is the same for every part. Nothing has to cross between parts.
All inputs are finite; a program needn't handle non-finite values.
Results may differ from a plain program's by a relative error of at most 0.0051.
Values may be sent and summed in bfloat16 or wider, within the bound.
A program may use at most 192 MiB of HBM per device.

v0:
```python
import jax
import jax.numpy as jnp
from jax import lax
from jax.sharding import PartitionSpec as P


def rms_scale(values, gain):
    mean_square = jnp.mean(values * values, axis=-1, keepdims=True)
    return values * lax.rsqrt(mean_square + 1e-05) * gain


def second_section(columns, left_factor):
    mixed = jnp.einsum("jia,sajc->sijc", left_factor, columns, preferred_element_type=jnp.float32)
    return mixed.astype(jnp.bfloat16)


def body(
    tokens, right_factor, left_factor, twiddle, norm_gain, mix_gain, value_weight, gate_weight
):
    seqs_here, rows_here, width = tokens.shape
    blocks_here = right_factor.shape[0]
    block_len = right_factor.shape[1]
    widened = tokens.astype(jnp.float32)
    normed = rms_scale(widened, norm_gain).astype(jnp.bfloat16)
    blocked = normed.reshape(seqs_here, blocks_here, block_len, width)
    section_one = jnp.einsum(
        "ajb,sabc->sajc", right_factor, blocked, preferred_element_type=jnp.float32
    )
    section_one = (section_one * twiddle[None, :, :, None]).astype(jnp.bfloat16)
    columns = lax.all_to_all(section_one, "seq", split_axis=2, concat_axis=1, tiled=True)
    mixed_cols = second_section(columns, left_factor)
    mixed_back = lax.all_to_all(mixed_cols, "seq", split_axis=1, concat_axis=2, tiled=True)
    residual_sum = widened + mixed_back.reshape(seqs_here, rows_here, width).astype(jnp.float32)
    mix_normed = (
        rms_scale(residual_sum, mix_gain).astype(jnp.bfloat16).reshape(seqs_here * rows_here, width)
    )
    values_out = jnp.dot(mix_normed, value_weight, preferred_element_type=jnp.float32)
    gates = jnp.dot(mix_normed, gate_weight, preferred_element_type=jnp.float32)
    gated = (values_out * jax.nn.sigmoid(gates)).reshape(seqs_here, rows_here, width)
    return (residual_sum + gated).astype(jnp.bfloat16)


def solution(mesh):
    return jax.shard_map(
        body,
        mesh=mesh,
        in_specs=(
            P("grp", "seq", None),
            P("seq", None, None),
            P("seq", None, None),
            P("seq", None),
            P(),
            P(),
            P(),
            P(),
        ),
        out_specs=P("grp", "seq", None),
        check_vma=False,
    )
```

profile of v0, /device:TPU:1, one launch (start us, length us, event | category | flops | bytes accessed | tf_op | source)
XLA Modules:
  0.0 759.3 jit_solution(9899287681793575877)
XLA Ops:
  0.0 0.0 copy-start
  0.0 0.0 copy-start.2
  0.0 7.2 fusion
  7.2 0.0 copy-done.2
  7.3 0.0 copy-start.4
  7.3 11.8 %fusion.2 = bf16[1,8192,768]{2,1,0:T(8,128)(2,1)} fusion(bf16[1,8192,768]{2,1,0:T(8,128)(2,1)} %param.8, f32[768]{0:T(1024)S(1)} %copy-done.2, f32[8192]{0:T(1024)S(1)} %add_rsqrt_fusion.1), kind=kLoop, calls=%fused_computation.5 | loop fusion | flops 25165824 | bytes 25201664 | tf_op jit(solution)/shard_map/convert_element_type | solution.py:24
  19.1 0.0 copy-done.4
  19.1 16.0 %fusion.9 = bf16[1,16,512,768]{2,3,1,0:T(8,128)(2,1)} fusion(f32[16,512]{1,0:T(8,128)S(1)} %copy-done.4, bf16[16,512,768]{2,1,0:T(8,128)(2,1)} %bitcast.45, bf16[16,512,512]{2,1,0:T(8,128)(2,1)} %param.9), kind=kOutput, calls=%fused_computation.15 | convolution fusion | flops 6455033856 | bytes 33587200 | tf_op jit(solution)/shard_map/ajb,sabc->sajc/dot_general | solution.py:26
  35.1 17.6 %copy.19 = bf16[1,16,512,768]{3,1,0,2:T(8,128)(2,1)} copy(bf16[1,16,512,768]{2,3,1,0:T(8,128)(2,1)} %fusion.9) | data formatting | bytes 25165824 | tf_op jit(solution)/shard_map/convert_element_type | solution.py:29
  52.7 279.7 %all_to_all.24 = bf16[1,16,512,768]{3,1,0,2:T(8,128)(2,1)S(1)} all-to-all(bf16[1,16,512,768]{3,1,0,2:T(8,128)(2,1)} %copy.19), channel_id=1, replica_groups=mesh['grp'=2,'seq'=16] {'seq'}, dimensions={2} | all-to-all | bytes 25165824 | tf_op jit(solution)/shard_map/all_to_all | solution.py:30
  332.4 8.8 %copy.20 = bf16[1,16,512,768]{3,2,1,0:T(8,128)(2,1)S(1)} copy(bf16[1,16,512,768]{3,1,0,2:T(8,128)(2,1)S(1)} %all_to_all.24) | data formatting | bytes 25165824 | tf_op jit(solution)/shard_map/all_to_all | solution.py:30
  341.3 5.3 copy.21
  346.6 18.1 %convert_bitcast_fusion.1 = bf16[1,256,32,768]{1,3,2,0:T(8,128)(2,1)} fusion(bf16[32,256,256]{2,1,0:T(8,128)(2,1)} %param.10, bf16[256,32,768]{2,1,0:T(8,128)(2,1)} %bitcast.44), kind=kOutput, calls=%fused_computation.22 | convolution fusion | flops 3227516928 | bytes 29360128 | tf_op jit(solution)/shard_map/jia,sajc->sijc/dot_general | solution.py:13
  364.7 16.6 %copy.23 = bf16[1,256,32,768]{3,2,0,1:T(8,128)(2,1)} copy(bf16[1,256,32,768]{1,3,2,0:T(8,128)(2,1)} %convert_bitcast_fusion.1) | data formatting | bytes 25165824 | tf_op jit(solution)/shard_map/convert_element_type | solution.py:14
  381.3 278.1 %all_to_all.25 = bf16[1,256,32,768]{3,2,0,1:T(8,128)(2,1)S(1)} all-to-all(bf16[1,256,32,768]{3,2,0,1:T(8,128)(2,1)} %copy.23), channel_id=1, replica_groups=mesh['grp'=2,'seq'=16] {'seq'}, dimensions={1} | all-to-all | bytes 25165824 | tf_op jit(solution)/shard_map/all_to_all | solution.py:32
  659.4 0.0 slice-start
  659.4 0.0 slice-start.1
  659.4 10.6 %convert_bitcast_fusion = f32[1,16,16,32,768]{4,3,1,2,0:T(8,128)} fusion(bf16[1,16,16,32,768]{4,3,2,1,0:T(8,128)(2,1)S(1)} %bitcast.43), kind=kLoop, calls=%fused_computation.6 | loop fusion | flops 6291456 | bytes 37748736 | tf_op jit(solution)/shard_map/convert_element_type | solution.py:33
  670.0 0.0 slice-start.2
  670.0 18.3 %copy.25 = f32[1,16,16,32,768]{4,3,2,1,0:T(8,128)} copy(f32[1,16,16,32,768]{4,3,1,2,0:T(8,128)} %convert_bitcast_fusion) | data formatting | bytes 50331648 | tf_op jit(solution)/shard_map/convert_element_type | solution.py:33
  688.3 0.0 slice-done
  688.3 0.0 slice-done.1
  688.3 0.0 slice-done.2
  688.3 0.0 copy-start.5
  688.3 17.8 %multiply_reduce_fusion = (f32[8192]{0:T(1024)S(1)}, f32[1,8192,768]{2,1,0:T(8,128)}) fusion(f32[1,16,16,32,768]{4,3,2,1,0:T(8,128)} %copy.25, bf16[1,8192,768]{2,1,0:T(8,128)(2,1)S(1)} %bitcast.41), kind=kLoop, calls=%fused_computation.12 | loop fusion | flops 25157632 | bytes 62947328 | tf_op jit(solution)/shard_map/reduce_sum | solution.py:8
  706.1 0.0 copy-done
  706.1 0.0 copy-done.5
  706.1 0.0 copy-start.3
  706.1 19.5 %fusion.7 = f32[8192,768]{1,0:T(8,128)} fusion(bf16[768,768]{1,0:T(8,128)(2,1)S(1)} %copy-done, f32[1,8192,768]{2,1,0:T(8,128)} %get-tuple-element.6, f32[768]{0:T(1024)S(1)} %copy-done.5, f32[8192]{0:T(1024)S(1)} %add_rsqrt_fusion), kind=kOutput, calls=%fused_computation.14 | convolution fusion | flops 9682550784 | bytes 51547136 | tf_op jit(solution)/shard_map/dot_general | solution.py:37
  725.6 0.0 copy-done.3
  725.6 33.6 %fusion.3 = bf16[1,8192,768]{2,1,0:T(8,128)(2,1)} fusion(f32[1,8192,768]{2,1,0:T(8,128)} %get-tuple-element.6, f32[8192,768]{1,0:T(8,128)} %fusion.7, bf16[768,768]{1,0:T(8,128)(2,1)S(1)} %copy-done.3, f32[768]{0:T(1024)S(1)} %copy-done.5, f32[8192]{0:T(1024)S(1)} %add_rsqrt_fusion), kind=kOutput, calls=%fused_computation.8 | convolution fusion | flops 9720299520 | bytes 64130048 | tf_op jit(solution)/shard_map/dot_general | solution.py:38
  759.3 0.0 copy-done.1
  (4 shorter events, 0.0 us)
Async XLA Ops:
  0.0 706.1 %copy-start = (bf16[768,768]{1,0:T(8,128)(2,1)S(1)}, bf16[768,768]{1,0:T(8,128)(2,1)}, u32[]{:S(2)}) copy-start(bf16[768,768]{1,0:T(8,128)(2,1)} %param.14) | copy-start | bytes 3538948
  0.0 7.2 copy-start.2
  7.3 11.8 %copy-start.4 = (f32[16,512]{1,0:T(8,128)S(1)}, f32[16,512]{1,0:T(8,128)}, u32[]{:S(2)}) copy-start(f32[16,512]{1,0:T(8,128)} %param.11) | copy-start | bytes 98308
  659.4 28.9 %slice-start = ((s8[12582912]{0:T(1024)(128)(4,1)}), s8[4194304]{0:T(1024)(128)(4,1)S(1)}, s32[]{:S(2)}) async-start(s8[12582912]{0:T(1024)(128)(4,1)} %bitcast.40), calls=%async_computation.2 | async-start | bytes 8388608
  659.4 28.9 %slice-start.1 = ((s8[12582912]{0:T(1024)(128)(4,1)}), s8[4194304]{0:T(1024)(128)(4,1)S(1)}, s32[]{:S(2)}) async-start(s8[12582912]{0:T(1024)(128)(4,1)} %bitcast.40), calls=%async_computation.3 | async-start | bytes 8388608
  670.0 18.3 %slice-start.2 = ((s8[12582912]{0:T(1024)(128)(4,1)}), s8[4194304]{0:T(1024)(128)(4,1)S(1)}, s32[]{:S(2)}) async-start(s8[12582912]{0:T(1024)(128)(4,1)} %bitcast.40), calls=%async_computation.4 | async-start | bytes 8388608
  688.3 17.8 %copy-start.5 = (f32[768]{0:T(1024)S(1)}, f32[768]{0:T(1024)}, u32[]{:S(2)}) copy-start(f32[768]{0:T(1024)} %param.13) | copy-start | bytes 9220
  706.1 19.5 %copy-start.3 = (bf16[768,768]{1,0:T(8,128)(2,1)S(1)}, bf16[768,768]{1,0:T(8,128)(2,1)}, u32[]{:S(2)}) copy-start(bf16[768,768]{1,0:T(8,128)(2,1)} %param.15) | copy-start | bytes 3538948
  725.6 33.6 %copy-start.1 = (bf16[768,768]{1,0:T(8,128)(2,1)S(1)}, bf16[768,768]{1,0:T(8,128)(2,1)}, u32[]{:S(2)}) copy-start(bf16[768,768]{1,0:T(8,128)(2,1)} %param.14) | copy-start | bytes 3538948
where the time goes:
time: 760 us; the launch traced here: 759 us
  blocking collectives  558 us (73%)
  matrix products  87.2 us (11%)
  local copies, waits for them, and re-layouts  66.6 us (9%)
  other arithmetic  47.4 us (6%)
    all_to_all x1, blocking collectives, body(): lax.all_to_all(section_one, 'seq', split_axis=2, concat_axis=1, tiled=True)  280 us
    all_to_all x1, blocking collectives, body(): lax.all_to_all(mixed_cols, 'seq', split_axis=1, concat_axis=2, tiled=True)  278 us
    dot_general x1, matrix products, body(): gates = jnp.dot(mix_normed, gate_weight, preferred_element_type=jnp.float32)  33.6 us
    reduce_sum x2, other arithmetic, rms_scale(): mean_square = jnp.mean(values * values, axis=-1, keepdims=True)  25 us
    dot_general x1, matrix products, body(): jnp.dot(mix_normed, value_weight, preferred_element_type=jnp.float32)  19.5 us
    convert_element_type x1, local copies, waits for them, and re-layouts, body(): mixed_back.reshape(seqs_here, rows_here, width).astype(jnp.float32)  18.3 us
    dot_general x1, matrix products, second_section(): jnp.einsum('jia,sajc->sijc', left_factor, columns, preferred_element_type...  18.1 us
    convert_element_type x1, local copies, waits for them, and re-layouts, body(): section_one = (section_one * twiddle[None, :, :, None]).astype(jnp.bfloat16)  17.6 us

commit v1 on v0

--- a/solution.py
+++ b/solution.py
@@ -2,6 +2,22 @@
 import jax.numpy as jnp
 from jax import lax
 from jax.sharding import PartitionSpec as P
+
+
+def exchange_in_pairs(array, axis, split, join):
+    ways, here = (lax.axis_size(axis), lax.axis_index(axis))
+    width = array.shape[split] // ways
+    lengths = list(array.shape)
+    lengths[split] = width
+    height = lengths[join]
+    lengths[join] = height * ways
+    full = jnp.zeros(lengths, array.dtype)
+    for mask in range(ways):
+        part = lax.dynamic_slice_in_dim(array, (here ^ mask) * width, width, axis=split)
+        if mask:
+            part = lax.ppermute(part, axis, [(d, d ^ mask) for d in range(ways)])
+        full = lax.dynamic_update_slice_in_dim(full, part, (here ^ mask) * height, axis=join)
+    return full
 
 
 def rms_scale(values, gain):
@@ -29,7 +45,7 @@
     section_one = (section_one * twiddle[None, :, :, None]).astype(jnp.bfloat16)
     columns = lax.all_to_all(section_one, "seq", split_axis=2, concat_axis=1, tiled=True)
     mixed_cols = second_section(columns, left_factor)
-    mixed_back = lax.all_to_all(mixed_cols, "seq", split_axis=1, concat_axis=2, tiled=True)
+    mixed_back = exchange_in_pairs(mixed_cols, "seq", 1, 2)
     residual_sum = widened + mixed_back.reshape(seqs_here, rows_here, width).astype(jnp.float32)
     mix_normed = (
         rms_scale(residual_sum, mix_gain).astype(jnp.bfloat16).reshape(seqs_here * rows_here, width)

time: 760 us -> 751 us (0.988)
  the two profiles are of different devices: /device:TPU:1 before, /device:TPU:13 now
where the time goes in v1:
time: 751 us; the launch traced here: 750 us
  waiting for transfers between devices  497 us (66%)
  matrix products  90 us (12%)
  local copies, waits for them, and re-layouts  86.4 us (12%)
  starting transfers between devices  49 us (7%)
  other arithmetic  27.3 us (4%)
    all_to_all x1, waiting for transfers between devices, body(): lax.all_to_all(section_one, 'seq', split_axis=2, concat_axis=1, tiled=True)  272 us
    ppermute x15, waiting for transfers between devices, exchange_in_pairs(): part = lax.ppermute(part, axis, [(d, d ^ mask) for d in range(ways)])  225 us
    ppermute x15, starting transfers between devices, exchange_in_pairs(): part = lax.ppermute(part, axis, [(d, d ^ mask) for d in range(ways)])  42.4 us
    dot_general x1, matrix products, body(): gates = jnp.dot(mix_normed, gate_weight, preferred_element_type=jnp.float32)  38.6 us
    all_to_all x2, local copies, waits for them, and re-layouts, body(): lax.all_to_all(section_one, 'seq', split_axis=2, concat_axis=1, tiled=True)  29.6 us
    dynamic_update_slice x16, local copies, waits for them, and re-layouts, exchange_in_pairs(): lax.dynamic_update_slice_in_dim(full, part, (here ^ mask) * height, axis=...  24.5 us
    dot_general x1, matrix products, body(): jnp.dot(mix_normed, value_weight, preferred_element_type=jnp.float32)  21.4 us
    convert_element_type x1, local copies, waits for them, and re-layouts, body(): section_one = (section_one * twiddle[None, :, :, None]).astype(jnp.bfloat16)  17.6 us
  transfers between devices with their start and end apart: 16, of which 11 were waited for; matrix products, arithmetic and copies ran while one was open for 4% of the time, Pallas kernels for 0%

profile of v1, /device:TPU:13, one launch (start us, length us, event | category | flops | bytes accessed | tf_op | source)
XLA Modules:
  0.0 750.2 jit_solution(7188614443723958596)
XLA Ops:
  0.0 7.2 fusion
  7.3 11.8 %fusion.2 = bf16[1,8192,768]{2,1,0:T(8,128)(2,1)} fusion(bf16[1,8192,768]{2,1,0:T(8,128)(2,1)} %param.8, f32[768]{0:T(1024)S(1)} %copy-done.6, f32[8192]{0:T(1024)S(1)} %add_rsqrt_fusion.1), kind=kLoop, calls=%fused_computation.5 | loop fusion | flops 25165824 | bytes 25201664 | tf_op jit(solution)/shard_map/convert_element_type | solution.py:40
  19.1 16.2 %fusion.9 = bf16[1,16,512,768]{2,3,1,0:T(8,128)(2,1)} fusion(f32[16,512]{1,0:T(8,128)S(1)} %copy-done.8, bf16[16,512,768]{2,1,0:T(8,128)(2,1)} %bitcast.100, bf16[16,512,512]{2,1,0:T(8,128)(2,1)} %param.9), kind=kOutput, calls=%fused_computation.14 | convolution fusion | flops 6455033856 | bytes 33587200 | tf_op jit(solution)/shard_map/ajb,sabc->sajc/dot_general | solution.py:42
  35.3 17.6 %copy.31 = bf16[1,16,512,768]{3,1,0,2:T(8,128)(2,1)} copy(bf16[1,16,512,768]{2,3,1,0:T(8,128)(2,1)} %fusion.9) | data formatting | bytes 25165824 | tf_op jit(solution)/shard_map/convert_element_type | solution.py:45
  52.9 6.6 all-to-all-start
  59.4 272.2 %all-to-all-done = bf16[1,16,512,768]{3,1,0,2:T(8,128)(2,1)} async-done(((bf16[1,16,512,768]{3,1,0,2:T(8,128)(2,1)}), bf16[1,16,512,768]{3,1,0,2:T(8,128)(2,1)}, u32[]{:S(2)}, u32[]{:S(2)}) %all-to-all-start) | async-done | bytes 12582944 | tf_op jit(solution)/shard_map/all_to_all | solution.py:46
  331.6 7.9 %copy.32 = bf16[1,16,512,768]{3,2,1,0:T(8,128)(2,1)S(1)} copy(bf16[1,16,512,768]{3,1,0,2:T(8,128)(2,1)} %all-to-all-done) | data formatting | bytes 25165824 | tf_op jit(solution)/shard_map/all_to_all | solution.py:46
  339.6 21.7 %copy.33 = bf16[1,16,16,32,768]{4,2,1,3,0:T(8,128)(2,1)} copy(bf16[1,16,16,32,768]{4,3,1,2,0:T(8,128)(2,1)S(1)} %bitcast.99) | data formatting | bytes 25165824 | tf_op jit(solution)/shard_map/all_to_all | solution.py:46
  361.3 13.8 %convolution_convert_fusion = bf16[32,768,256]{1,2,0:T(8,128)(2,1)} fusion(bf16[32,256,256]{2,1,0:T(8,128)(2,1)} %param.10, bf16[256,32,768]{2,0,1:T(8,128)(2,1)} %bitcast.96), kind=kOutput, calls=%fused_computation.19 | convolution fusion | flops 3227516928 | bytes 29360128 | tf_op jit(solution)/shard_map/jia,sajc->sijc/dot_general | solution.py:29
  375.1 8.8 %dynamic-slice_bitcast_fusion = (bf16[1,16,32,768]{3,1,0,2:T(8,128)(2,1)S(1)}, bf16[1,16,32,768]{3,1,0,2:T(8,128)(2,1)S(1)}, bf16[1,16,32,768]{3,1,0,2:T(8,128)(...) fusion(bf16[32,768,256]{1,2,0:T(8,128)(2,1)} %convolution_conve, ...), kind=kLoop, calls=%fused_computation.36 | loop fusion | bytes 25165888 | tf_op jit(solution)/shard_map/dynamic_slice | solution.py:16
  388.6 5.8 broadcast_in_dim.2
  395.6 2.7 copy_dynamic-update-slice_fusion.14
  398.3 5.3 collective-permute-done.1
  403.5 2.3 copy_dynamic-update-slice_fusion.13
  405.8 15.3 %collective-permute-done.2 = bf16[1,16,32,768]{3,1,0,2:T(8,128)(2,1)} collective-permute-done((bf16[1,16,32,768]{3,1,0,2:T(8,128)(2,1)}, bf16[1,16,32,768]{3,1,0,2:T(8,128)(2,1)}, u32[]{:S(2)}, u32[]{:S(2)}) %collective-permute-start.2) | collective-permute-done | bytes 786464 | tf_op jit(solution)/shard_map/ppermute | solution.py:18
  421.1 18.2 %collective-permute-start.5 = (bf16[1,16,32,768]{3,1,0,2:T(8,128)(2,1)}, bf16[1,16,32,768]{3,1,0,2:T(8,128)(2,1)S(1)}, u32[]{:S(2)}, u32[]{:S(2)}) collective-permute-start(bf16[1,16,32,768]{3,1,0,2:T(8,128)(2,1)} %get-tuple-element.14), channel_id=1, source_target_pairs={{0,6},{1,7},{2,4},{3,5},{4,2},{5,3},{6,0},{7,1},{8,14},{9,15},{10,... | collective-permute-start | bytes 2359304 | tf_op jit(solution)/shard_map/ppermute | solution.py:18
  439.3 2.3 copy_dynamic-update-slice_fusion.12
  443.0 14.0 %collective-permute-done.4 = bf16[1,16,32,768]{3,1,0,2:T(8,128)(2,1)S(1)} collective-permute-done((bf16[1,16,32,768]{3,1,0,2:T(8,128)(2,1)}, bf16[1,16,32,768]{3,1,0,2:T(8,128)(2,1)S(1)}, u32[]{:S(2)}, u32[]{:S(2)}) %collective-permute-start.4) | collective-permute-done | bytes 786464 | tf_op jit(solution)/shard_map/ppermute | solution.py:18
  457.0 4.4 collective-permute-start.7
  462.5 24.4 %collective-permute-done.5 = bf16[1,16,32,768]{3,1,0,2:T(8,128)(2,1)S(1)} collective-permute-done((bf16[1,16,32,768]{3,1,0,2:T(8,128)(2,1)}, bf16[1,16,32,768]{3,1,0,2:T(8,128)(2,1)S(1)}, u32[]{:S(2)}, u32[]{:S(2)}) %collective-permute-start.5) | collective-permute-done | bytes 786464 | tf_op jit(solution)/shard_map/ppermute | solution.py:18
  486.9 6.8 collective-permute-start.8
  494.8 9.0 %collective-permute-done.6 = bf16[1,16,32,768]{3,1,0,2:T(8,128)(2,1)S(1)} collective-permute-done((bf16[1,16,32,768]{3,1,0,2:T(8,128)(2,1)}, bf16[1,16,32,768]{3,1,0,2:T(8,128)(2,1)S(1)}, u32[]{:S(2)}, u32[]{:S(2)}) %collective-permute-start.6) | collective-permute-done | bytes 786464 | tf_op jit(solution)/shard_map/ppermute | solution.py:18
  503.8 6.6 collective-permute-start.9
  513.1 60.8 %collective-permute-done.8 = bf16[1,16,32,768]{3,1,0,2:T(8,128)(2,1)S(1)} collective-permute-done((bf16[1,16,32,768]{3,1,0,2:T(8,128)(2,1)}, bf16[1,16,32,768]{3,1,0,2:T(8,128)(2,1)S(1)}, u32[]{:S(2)}, u32[]{:S(2)}) %collective-permute-start.8) | collective-permute-done | bytes 786464 | tf_op jit(solution)/shard_map/ppermute | solution.py:18
  575.5 32.0 %collective-permute-done.9 = bf16[1,16,32,768]{3,1,0,2:T(8,128)(2,1)S(1)} collective-permute-done((bf16[1,16,32,768]{3,1,0,2:T(8,128)(2,1)S(1)}, bf16[1,16,32,768]{3,1,0,2:T(8,128)(2,1)S(1)}, u32[]{:S(2)}, u32[]{:S(2)}) %collective-permute-start.9) | collective-permute-done | bytes 786464 | tf_op jit(solution)/shard_map/ppermute | solution.py:18
  609.4 31.9 %collective-permute-done.10 = bf16[1,16,32,768]{3,1,0,2:T(8,128)(2,1)S(1)} collective-permute-done((bf16[1,16,32,768]{3,1,0,2:T(8,128)(2,1)S(1)}, bf16[1,16,32,768]{3,1,0,2:T(8,128)(2,1)S(1)}, u32[]{:S(2)}, u32[]{:S(2)}) %collective-permute-start.10) | collective-permute-done | bytes 786464 | tf_op jit(solution)/shard_map/ppermute | solution.py:18
  642.5 16.8 %collective-permute-done.11 = bf16[1,16,32,768]{3,1,0,2:T(8,128)(2,1)S(1)} collective-permute-done((bf16[1,16,32,768]{3,1,0,2:T(8,128)(2,1)S(1)}, bf16[1,16,32,768]{3,1,0,2:T(8,128)(2,1)S(1)}, u32[]{:S(2)}, u32[]{:S(2)}) %collective-permute-start.11) | collective-permute-done | bytes 786464 | tf_op jit(solution)/shard_map/ppermute | solution.py:18
  660.4 15.7 %collective-permute-done.12 = bf16[1,16,32,768]{3,1,0,2:T(8,128)(2,1)S(1)} collective-permute-done((bf16[1,16,32,768]{3,1,0,2:T(8,128)(2,1)S(1)}, bf16[1,16,32,768]{3,1,0,2:T(8,128)(2,1)S(1)}, u32[]{:S(2)}, u32[]{:S(2)}) %collective-permute-start.12) | collective-permute-done | bytes 786464 | tf_op jit(solution)/shard_map/ppermute | solution.py:18
  679.5 2.3 copy_dynamic-update-slice_fusion
  681.9 8.2 %multiply_reduce_fusion = f32[8192]{0:T(1024)S(1)} fusion(bf16[1,8192,768]{2,1,0:T(8,128)(2,1)S(1)} %bitcast.95, bf16[1,16,512,768]{3,2,1,0:T(8,128)(2,1)} %copy_dynamic-update-slice_fusion), kind=kLoop, calls=%fused_computation.11 | loop fusion | flops 31449088 | bytes 25198592 | tf_op jit(solution)/shard_map/reduce_sum | solution.py:24
  690.2 21.4 %fusion.7 = f32[8192,768]{1,0:T(8,128)} fusion(bf16[768,768]{1,0:T(8,128)(2,1)S(1)} %copy-done, bf16[1,8192,768]{2,1,0:T(8,128)(2,1)} %bitcast.97, bf16[1,8192,768]{2,1,0:T(8,128)(2,1)} %param.8, f32[768]{0:T(1024)S(1)} %copy-done.9, f32[8192]{0:T(1024)S(1)} %add_rsqrt_fusion), kind=kOutput, calls=%fused_computation.13 | convolution fusion | flops 9701425152 | bytes 51547136 | tf_op jit(solution)/shard_map/dot_general | solution.py:53
  711.6 38.6 %fusion.3 = bf16[1,8192,768]{2,1,0:T(8,128)(2,1)} fusion(f32[8192,768]{1,0:T(8,128)} %fusion.7, bf16[1,8192,768]{2,1,0:T(8,128)(2,1)} %bitcast.98, bf16[1,8192,768]{2,1,0:T(8,128)(2,1)} %param.8, bf16[768,768]{1,0:T(8,128)(2,1)S(1)} %copy-done.7, f32[768]{0:T(1024)S(1)} %copy-done.9, f32[8192]{0:T(1024)S(1)} %add_rsqrt_fusion), kind=kOutput, calls=%fused_computation.7 | convolution fusion | flops 9758048256 | bytes 64130048 | tf_op jit(solution)/shard_map/dot_general | solution.py:54
  (57 shorter events, 21.4 us)
Async XLA Ops:
  0.0 690.2 %copy-start = (bf16[768,768]{1,0:T(8,128)(2,1)S(1)}, bf16[768,768]{1,0:T(8,128)(2,1)}, u32[]{:S(2)}) copy-start(bf16[768,768]{1,0:T(8,128)(2,1)} %param.14) | copy-start | bytes 3538948
  0.0 7.2 copy-start.6
  7.3 11.8 %copy-start.8 = (f32[16,512]{1,0:T(8,128)S(1)}, f32[16,512]{1,0:T(8,128)}, u32[]{:S(2)}) copy-start(f32[16,512]{1,0:T(8,128)} %param.11) | copy-start | bytes 98308
  52.9 278.8 %all-to-all-start = ((bf16[1,16,512,768]{3,1,0,2:T(8,128)(2,1)}), bf16[1,16,512,768]{3,1,0,2:T(8,128)(2,1)}, u32[]{:S(2)}, u32[]{:S(2)}) async-start(bf16[1,16,512,768]{3,1,0,2:T(8,128)(2,1)} %copy.31), calls=%async_computation | async-start | bytes 25165824 | tf_op jit(solution)/shard_map/all_to_all | solution.py:46
  383.9 11.7 %collective-permute-start = (bf16[1,16,32,768]{3,1,0,2:T(8,128)(2,1)}, bf16[1,16,32,768]{3,1,0,2:T(8,128)(2,1)}, u32[]{:S(2)}, u32[]{:S(2)}) collective-permute-start(bf16[1,16,32,768]{3,1,0,2:T(8,128)(2,1)} %get-tuple-element.19), channel_id=1, source_target_pairs={{0,1},{1,0},{2,3},{3,2},{4,5},{5,4},{6,7},{7,6},{8,9},{9,8},{10,11... | collective-permute-start | bytes 2359304 | tf_op jit(solution)/shard_map/ppermute | solution.py:18
  384.2 19.3 %collective-permute-start.1 = (bf16[1,16,32,768]{3,1,0,2:T(8,128)(2,1)}, bf16[1,16,32,768]{3,1,0,2:T(8,128)(2,1)}, u32[]{:S(2)}, u32[]{:S(2)}) collective-permute-start(bf16[1,16,32,768]{3,1,0,2:T(8,128)(2,1)} %get-tuple-element.18), channel_id=1, source_target_pairs={{0,2},{1,3},{2,0},{3,1},{4,6},{5,7},{6,4},{7,5},{8,10},{9,11},{10,... | collective-permute-start | bytes 2359304 | tf_op jit(solution)/shard_map/ppermute | solution.py:18
  384.2 119.6 %copy-start.5 = (bf16[1,16,32,768]{3,1,0,2:T(8,128)(2,1)S(1)}, bf16[1,16,32,768]{3,1,0,2:T(8,128)(2,1)}, u32[]{:S(2)}) copy-start(bf16[1,16,32,768]{3,1,0,2:T(8,128)(2,1)} %get-tuple-element.10) | copy-start | bytes 2359300
  384.2 295.3 %collective-permute-start.14 = (bf16[1,16,32,768]{3,1,0,2:T(8,128)(2,1)S(1)}, bf16[1,16,32,768]{3,1,0,2:T(8,128)(2,1)}, u32[]{:S(2)}, u32[]{:S(2)}) collective-permute-start(bf16[1,16,32,768]{3,1,0,2:T(8,128)(2,1)S(1)} %get-tuple-element.5), channel_id=1, source_target_pairs={{0,15},{1,14},{2,13},{3,12},{4,11},{5,10},{6,9},{7,8},{8,7},{9,6},... | collective-permute-start | bytes 2359304 | tf_op jit(solution)/shard_map/ppermute | solution.py:18
  385.9 291.4 %collective-permute-start.13 = (bf16[1,16,32,768]{3,1,0,2:T(8,128)(2,1)S(1)}, bf16[1,16,32,768]{3,1,0,2:T(8,128)(2,1)}, u32[]{:S(2)}, u32[]{:S(2)}) collective-permute-start(bf16[1,16,32,768]{3,1,0,2:T(8,128)(2,1)S(1)} %get-tuple-element.6), channel_id=1, source_target_pairs={{0,14},{1,15},{2,12},{3,13},{4,10},{5,11},{6,8},{7,9},{8,6},{9,7},... | collective-permute-start | bytes 2359304 | tf_op jit(solution)/shard_map/ppermute | solution.py:18
  386.7 34.4 %collective-permute-start.2 = (bf16[1,16,32,768]{3,1,0,2:T(8,128)(2,1)}, bf16[1,16,32,768]{3,1,0,2:T(8,128)(2,1)}, u32[]{:S(2)}, u32[]{:S(2)}) collective-permute-start(bf16[1,16,32,768]{3,1,0,2:T(8,128)(2,1)} %get-tuple-element.17), channel_id=1, source_target_pairs={{0,3},{1,2},{2,1},{3,0},{4,7},{5,6},{6,5},{7,4},{8,11},{9,10},{10,... | collective-permute-start | bytes 2359304 | tf_op jit(solution)/shard_map/ppermute | solution.py:18
  388.6 123.1 %copy-start.4 = (bf16[1,16,32,768]{3,1,0,2:T(8,128)(2,1)S(1)}, bf16[1,16,32,768]{3,1,0,2:T(8,128)(2,1)}, u32[]{:S(2)}) copy-start(bf16[1,16,32,768]{3,1,0,2:T(8,128)(2,1)} %get-tuple-element.9) | copy-start | bytes 2359300
  388.6 185.4 %copy-start.3 = (bf16[1,16,32,768]{3,1,0,2:T(8,128)(2,1)S(1)}, bf16[1,16,32,768]{3,1,0,2:T(8,128)(2,1)}, u32[]{:S(2)}) copy-start(bf16[1,16,32,768]{3,1,0,2:T(8,128)(2,1)} %get-tuple-element.8) | copy-start | bytes 2359300
  388.6 219.0 %copy-start.2 = (bf16[1,16,32,768]{3,1,0,2:T(8,128)(2,1)S(1)}, bf16[1,16,32,768]{3,1,0,2:T(8,128)(2,1)}, u32[]{:S(2)}) copy-start(bf16[1,16,32,768]{3,1,0,2:T(8,128)(2,1)} %get-tuple-element.7) | copy-start | bytes 2359300
  394.4 287.5 %slice-start = ((s8[12582912]{0:T(1024)(128)(4,1)}), s8[4194304]{0:T(1024)(128)(4,1)S(1)}, s32[]{:S(2)}) async-start(s8[12582912]{0:T(1024)(128)(4,1)} %bitcast.94), calls=%async_computation.1 | async-start | bytes 8388608
  395.6 46.0 %collective-permute-start.3 = (bf16[1,16,32,768]{3,1,0,2:T(8,128)(2,1)}, bf16[1,16,32,768]{3,1,0,2:T(8,128)(2,1)S(1)}, u32[]{:S(2)}, u32[]{:S(2)}) collective-permute-start(bf16[1,16,32,768]{3,1,0,2:T(8,128)(2,1)} %get-tuple-element.16), channel_id=1, source_target_pairs={{0,4},{1,5},{2,6},{3,7},{4,0},{5,1},{6,2},{7,3},{8,12},{9,13},{10,... | collective-permute-start | bytes 2359304 | tf_op jit(solution)/shard_map/ppermute | solution.py:18
  403.5 53.5 %collective-permute-start.4 = (bf16[1,16,32,768]{3,1,0,2:T(8,128)(2,1)}, bf16[1,16,32,768]{3,1,0,2:T(8,128)(2,1)S(1)}, u32[]{:S(2)}, u32[]{:S(2)}) collective-permute-start(bf16[1,16,32,768]{3,1,0,2:T(8,128)(2,1)} %get-tuple-element.15), channel_id=1, source_target_pairs={{0,5},{1,4},{2,7},{3,6},{4,1},{5,0},{6,3},{7,2},{8,13},{9,12},{10,... | collective-permute-start | bytes 2359304 | tf_op jit(solution)/shard_map/ppermute | solution.py:18
  421.1 65.7 %collective-permute-start.5 = (bf16[1,16,32,768]{3,1,0,2:T(8,128)(2,1)}, bf16[1,16,32,768]{3,1,0,2:T(8,128)(2,1)S(1)}, u32[]{:S(2)}, u32[]{:S(2)}) collective-permute-start(bf16[1,16,32,768]{3,1,0,2:T(8,128)(2,1)} %get-tuple-element.14), channel_id=1, source_target_pairs={{0,6},{1,7},{2,4},{3,5},{4,2},{5,3},{6,0},{7,1},{8,14},{9,15},{10,... | collective-permute-start | bytes 2359304 | tf_op jit(solution)/shard_map/ppermute | solution.py:18
  441.6 62.2 %collective-permute-start.6 = (bf16[1,16,32,768]{3,1,0,2:T(8,128)(2,1)}, bf16[1,16,32,768]{3,1,0,2:T(8,128)(2,1)S(1)}, u32[]{:S(2)}, u32[]{:S(2)}) collective-permute-start(bf16[1,16,32,768]{3,1,0,2:T(8,128)(2,1)} %get-tuple-element.13), channel_id=1, source_target_pairs={{0,7},{1,6},{2,5},{3,4},{4,3},{5,2},{6,1},{7,0},{8,15},{9,14},{10,... | collective-permute-start | bytes 2359304 | tf_op jit(solution)/shard_map/ppermute | solution.py:18
  457.0 224.9 %slice-start.1 = ((s8[12582912]{0:T(1024)(128)(4,1)}), s8[4194304]{0:T(1024)(128)(4,1)S(1)}, s32[]{:S(2)}) async-start(s8[12582912]{0:T(1024)(128)(4,1)} %bitcast.94), calls=%async_computation.2 | async-start | bytes 8388608
  457.0 54.7 %collective-permute-start.7 = (bf16[1,16,32,768]{3,1,0,2:T(8,128)(2,1)}, bf16[1,16,32,768]{3,1,0,2:T(8,128)(2,1)S(1)}, u32[]{:S(2)}, u32[]{:S(2)}) collective-permute-start(bf16[1,16,32,768]{3,1,0,2:T(8,128)(2,1)} %get-tuple-element.12), channel_id=1, source_target_pairs={{0,8},{1,9},{2,10},{3,11},{4,12},{5,13},{6,14},{7,15},{8,0},{9,1},... | collective-permute-start | bytes 2359304 | tf_op jit(solution)/shard_map/ppermute | solution.py:18
  486.9 87.1 %collective-permute-start.8 = (bf16[1,16,32,768]{3,1,0,2:T(8,128)(2,1)}, bf16[1,16,32,768]{3,1,0,2:T(8,128)(2,1)S(1)}, u32[]{:S(2)}, u32[]{:S(2)}) collective-permute-start(bf16[1,16,32,768]{3,1,0,2:T(8,128)(2,1)} %get-tuple-element.11), channel_id=1, source_target_pairs={{0,9},{1,8},{2,11},{3,10},{4,13},{5,12},{6,15},{7,14},{8,1},{9,0},... | collective-permute-start | bytes 2359304 | tf_op jit(solution)/shard_map/ppermute | solution.py:18
  503.8 103.7 %collective-permute-start.9 = (bf16[1,16,32,768]{3,1,0,2:T(8,128)(2,1)S(1)}, bf16[1,16,32,768]{3,1,0,2:T(8,128)(2,1)S(1)}, u32[]{:S(2)}, u32[]{:S(2)}) collective-permute-start(bf16[1,16,32,768]{3,1,0,2:T(8,128)(2,1)S(1)} %copy-done.5), channel_id=1, source_target_pairs={{0,10},{1,11},{2,8},{3,9},{4,14},{5,15},{6,12},{7,13},{8,2},{9,3},... | collective-permute-start | bytes 2359304 | tf_op jit(solution)/shard_map/ppermute | solution.py:18
  511.7 129.6 %collective-permute-start.10 = (bf16[1,16,32,768]{3,1,0,2:T(8,128)(2,1)S(1)}, bf16[1,16,32,768]{3,1,0,2:T(8,128)(2,1)S(1)}, u32[]{:S(2)}, u32[]{:S(2)}) collective-permute-start(bf16[1,16,32,768]{3,1,0,2:T(8,128)(2,1)S(1)} %copy-done.4), channel_id=1, source_target_pairs={{0,11},{1,10},{2,9},{3,8},{4,15},{5,14},{6,13},{7,12},{8,3},{9,2},... | collective-permute-start | bytes 2359304 | tf_op jit(solution)/shard_map/ppermute | solution.py:18
  574.0 85.3 %collective-permute-start.11 = (bf16[1,16,32,768]{3,1,0,2:T(8,128)(2,1)S(1)}, bf16[1,16,32,768]{3,1,0,2:T(8,128)(2,1)S(1)}, u32[]{:S(2)}, u32[]{:S(2)}) collective-permute-start(bf16[1,16,32,768]{3,1,0,2:T(8,128)(2,1)S(1)} %copy-done.3), channel_id=1, source_target_pairs={{0,12},{1,13},{2,14},{3,15},{4,8},{5,9},{6,10},{7,11},{8,4},{9,5},... | collective-permute-start | bytes 2359304 | tf_op jit(solution)/shard_map/ppermute | solution.py:18
  607.6 74.3 %slice-start.2 = ((s8[12582912]{0:T(1024)(128)(4,1)}), s8[4194304]{0:T(1024)(128)(4,1)S(1)}, s32[]{:S(2)}) async-start(s8[12582912]{0:T(1024)(128)(4,1)} %bitcast.94), calls=%async_computation.3 | async-start | bytes 8388608
  607.6 68.6 %collective-permute-start.12 = (bf16[1,16,32,768]{3,1,0,2:T(8,128)(2,1)S(1)}, bf16[1,16,32,768]{3,1,0,2:T(8,128)(2,1)S(1)}, u32[]{:S(2)}, u32[]{:S(2)}) collective-permute-start(bf16[1,16,32,768]{3,1,0,2:T(8,128)(2,1)S(1)} %copy-done.2), channel_id=1, source_target_pairs={{0,13},{1,12},{2,15},{3,14},{4,9},{5,8},{6,11},{7,10},{8,5},{9,4},... | collective-permute-start | bytes 2359304 | tf_op jit(solution)/shard_map/ppermute | solution.py:18
  681.9 8.3 %copy-start.9 = (f32[768]{0:T(1024)S(1)}, f32[768]{0:T(1024)}, u32[]{:S(2)}) copy-start(f32[768]{0:T(1024)} %param.13) | copy-start | bytes 9220
  690.2 21.4 %copy-start.7 = (bf16[768,768]{1,0:T(8,128)(2,1)S(1)}, bf16[768,768]{1,0:T(8,128)(2,1)}, u32[]{:S(2)}) copy-start(bf16[768,768]{1,0:T(8,128)(2,1)} %param.15) | copy-start | bytes 3538948
  711.6 38.6 %copy-start.1 = (bf16[768,768]{1,0:T(8,128)(2,1)S(1)}, bf16[768,768]{1,0:T(8,128)(2,1)}, u32[]{:S(2)}) copy-start(bf16[768,768]{1,0:T(8,128)(2,1)} %param.14) | copy-start | bytes 3538948
